TPU v7x, 32 devices: a whole 2x2x4 slice. The times are simulated.
32 devices in a mesh: lev: 2 (over x), gx: 8 (over z, y), gy: 2 (over core).
Axes of the slice: x: 2, y: 2, z: 4, core: 2. Of those that a mesh axis runs over, the one named last changes fastest.
Arguments:
- increments: float32 [1, 2, 80, 128, 256], P(None, None, 'lev', 'gx', 'gy'), may hold values from -6 to 6
- vert_corr: float32 [2, 80, 80], replicated, may hold values from -0.025 to 1, as said below
- kappa: float32 [2, 128, 256], P(None, 'gx', 'gy'), may hold values from 0.03 to 0.24
- sea_mask: int32 [80, 128, 256], P('lev', 'gx', 'gy'), may hold values 0 or 1
- level_count: int32 [128, 256], P('gx', 'gy'), may hold values from 10 to 75
Outputs:
- covaried: float32 [1, 2, 80, 128, 256], P(None, None, 'lev', 'gx', 'gy')
Inputs may be any that keep to these rules, and one draw needn't show every extreme that they name: vert_corr has ones on the diagonal, and each row's other entries together have magnitude below one.
All inputs are finite; a program needn't handle non-finite values. No bound on the sum of `sea_mask` on one device may be relied on, other than what follows from the above.
Results may differ from a plain program's by a relative error of at most 0.00021.
Values sent between devices are 32-bit elements; how exact they have to be, the bound alone decides.
A program may use at most 64 MiB of HBM per device.

v0:
```python
import jax
import jax.numpy as jnp
from jax import lax
from jax.sharding import PartitionSpec as P

PASSES = 10


def from_behind(block, axis, distance):
    devices = range(lax.axis_size(axis))
    route = [((i - distance) % len(devices), i) for i in devices]
    return lax.ppermute(block, axis, route)


def shifted(block, axis, distance):
    devices = range(lax.axis_size(axis))
    route = [(i - distance, i) for i in devices if i - distance in devices]
    return lax.ppermute(block, axis, route)


def padded(cells, sides, width):
    for axis, dim in sides:
        count = lax.axis_size(axis)
        head = lax.slice_in_dim(cells, 0, width, axis=dim)
        tail = lax.slice_in_dim(cells, cells.shape[dim] - width, cells.shape[dim], axis=dim)
        cells = jnp.concatenate(
            [
                lax.ppermute(tail, axis, [(i, (i + 1) % count) for i in range(count)]),
                cells,
                lax.ppermute(head, axis, [((i + 1) % count, i) for i in range(count)]),
            ],
            axis=dim,
        )
    return cells


def relax(extended, east_ext, north_ext, wet_center):
    center = extended[..., 1:-1, 1:-1]
    flux = east_ext[1:-1, 1:-1] * (extended[..., 2:, 1:-1] - center)
    flux = flux + east_ext[:-2, 1:-1] * (extended[..., :-2, 1:-1] - center)
    flux = flux + north_ext[1:-1, 1:-1] * (extended[..., 1:-1, 2:] - center)
    flux = flux + north_ext[1:-1, :-2] * (extended[..., 1:-1, :-2] - center)
    return wet_center * (center + flux)


def per_device(increments, vert_corr, kappa, sea_mask, level_count):
    lev_dev = sea_mask.shape[0]
    cells_x = sea_mask.shape[1]
    cells_y = sea_mask.shape[2]
    lev_first = lax.axis_index("lev") * lev_dev
    levels = lev_first + jnp.arange(lev_dev, dtype=jnp.int32)
    wet = sea_mask * (levels[:, None, None] < level_count[None]).astype(jnp.int32)
    wet_float = wet.astype(jnp.float32)
    masked = increments * wet_float
    own_rows = lax.dynamic_slice_in_dim(vert_corr, lev_first, lev_dev, 1)
    correlated = jnp.einsum(
        "toh,dthxy->dtoxy",
        own_rows,
        lax.all_gather(masked, "lev", axis=2, tiled=True),
        precision=lax.Precision.HIGHEST,
    )
    field = correlated * wet_float
    total_y = cells_y * lax.axis_size("gy")
    local_rows = lax.axis_index("gy") * cells_y + jnp.arange(cells_y, dtype=jnp.int32)
    open_local = (local_rows != total_y - 1).astype(jnp.float32)
    east_local = kappa[0]
    north_local = kappa[1] * open_local[None, :]
    east_low = from_behind(east_local[-1:, :], "gx", 1)
    north_low = shifted(north_local[:, -1:], "gy", 1)
    zero_row = jnp.zeros((1, cells_y), jnp.float32)
    zero_col = jnp.zeros((cells_x, 1), jnp.float32)
    east_ext = jnp.pad(jnp.concatenate([east_low, east_local, zero_row], axis=0), ((0, 0), (1, 1)))
    north_ext = jnp.pad(
        jnp.concatenate([north_low, north_local, zero_col], axis=1), ((1, 1), (0, 0))
    )

    def one_pass(step, current):
        extended = padded(current, (("gx", 3), ("gy", 4)), 1)
        return relax(extended, east_ext, north_ext, wet_float)

    field = lax.fori_loop(0, PASSES, one_pass, field)
    return field


def solution(mesh):
    in_specs = (
        P(None, None, "lev", "gx", "gy"),
        P(),
        P(None, "gx", "gy"),
        P("lev", "gx", "gy"),
        P("gx", "gy"),
    )
    out_specs = P(None, None, "lev", "gx", "gy")
    return jax.shard_map(
        per_device, mesh=mesh, in_specs=in_specs, out_specs=out_specs, check_vma=False
    )
```

profile of v0, /device:TPU:0, one launch (start us, length us, event | category | flops | bytes accessed | tf_op | source)
XLA Modules:
  0.0 171.8 jit_solution(11940098655885477659)
XLA Ops:
  6.5 1.1 fusion.21
  7.7 2.1 %copy_multiply_fusion = f32[1,2,40,16,128]{4,2,3,1,0:T(8,128)} fusion(f32[1,2,40,16,128]{4,3,2,1,0:T(8,128)} %param.7, f32[40,16,128]{2,0,1:T(8,128)S(1)} %fusion.21), kind=kLoop, calls=%fused_computation.24 | loop fusion | flops 163840 | bytes 1638400 | tf_op jit(solution)/shard_map/mul | solution.py:54
  9.9 3.0 %collective-permute-start.4 = (f32[1,128]{1,0:T(1,128)S(1)}, f32[1,128]{1,0:T(1,128)S(1)}, u32[]{:S(2)}, u32[]{:S(2)}) collective-permute-start(f32[1,128]{1,0:T(1,128)S(1)} %slice_bitcast_fusion.1), channel_id=1, source_target_pairs={{14,0},{0,2},{2,4},{4,6},{6,8},{8,10},{10,12},{12,14},{15,1},{1,3}... | collective-permute-start | bytes 1544 | tf_op jit(solution)/shard_map/ppermute | solution.py:12
  13.0 1.4 collective-permute-start.5
  14.6 0.7 collective-permute-done.5
  15.3 2.1 %collective-permute-done.4 = f32[1,128]{1,0:T(1,128)S(1)} collective-permute-done((f32[1,128]{1,0:T(1,128)S(1)}, f32[1,128]{1,0:T(1,128)S(1)}, u32[]{:S(2)}, u32[]{:S(2)}) %collective-permute-start.4) | collective-permute-done | bytes 544 | tf_op jit(solution)/shard_map/ppermute | solution.py:12
  17.6 19.4 %all-gather.2.cloned.1.call-done = f32[1,2,80,16,128]{4,2,3,1,0:T(8,128)} async-done(((f32[1,2,40,16,128]{4,2,3,1,0:T(8,128)}), f32[1,2,80,16,128]{4,2,3,1,0:T(8,128)}) %all-gather.2.cloned.1.call-update) | async-done | bytes 1310736 | tf_op jit(solution)/shard_map/all_gather | solution.py:59
  37.0 3.0 %fusion.18 = f32[1,2,40,16,128]{4,2,3,1,0:T(8,128)} fusion(f32[1,2,80,16,128]{4,2,3,1,0:T(8,128)} %all-gather.2.cloned.1.call-done, f32[40,16,128]{2,0,1:T(8,128)S(1)} %fusion.21, f32[2,80,80]{2,1,0:T(8,128)S(1)} %copy-done, s32[]{:T(128)S(6)} %select_n.3), kind=kOutput, calls=%fused_computation.23 | convolution fusion | flops 157450240 | bytes 2334724 | tf_op jit(solution)/shard_map/toh,dthxy->dtoxy/dot_general | solution.py:56
  40.0 122.9 %while.10 = (s32[]{:T(128)}, f32[1,2,40,16,128]{4,2,3,1,0:T(8,128)}, f32[40,16,128]{2,0,1:T(8,128)S(1)}, f32[18,130]{1,0:T(8,128)S(1)}, f32[18,130]{1,0:T(8,128)S(1)}, /*index=5*/s32[]{:T(128)}) while((s32[]{:T(128)}, f32[1,2,40,16,128]{4,2,3,1,0:T(8,128)}, f32[40,16,128]{2,0,1:T(8,128)S(1)}, f32[18,130]{1,0:T(8,128)S(1)}, ...), condition=%wide.region_1.2_spmd, body=%wide.region_0.1_spmd.sunk | while | flops 2785282 | bytes 5959653 | solution.py:81
  40.0 1.1 copy.47
  41.1 1.5 collective-permute-start
  42.6 3.2 %collective-permute-start.1 = (f32[1,2,40,1,128]{4,2,3,1,0:T(8,128)S(1)}, f32[1,2,40,1,128]{4,2,3,1,0:T(8,128)S(1)}, u32[]{:S(2)}, u32[]{:S(2)}) collective-permute-start(f32[1,2,40,1,128]{4,2,3,1,0:T(8,128)S(1)} %get-tuple-element.103), channel_id=1, source_target_pairs={{2,0},{4,2},{6,4},{8,6},{10,8},{12,10},{14,12},{0,14},{3,1},{5,3},... | collective-permute-start | bytes 122888 | tf_op jit(solution)/shard_map/while/body/eval_jaxpr/ppermute | solution.py:30
  45.8 2.0 %collective-permute-done = f32[1,2,40,1,128]{4,2,3,1,0:T(8,128)S(1)} collective-permute-done((f32[1,2,40,1,128]{4,2,3,1,0:T(8,128)S(1)}, f32[1,2,40,1,128]{4,2,3,1,0:T(8,128)S(1)}, u32[]{:S(2)}, u32[]{:S(2)}) %collective-permute-start) | collective-permute-done | bytes 40992 | tf_op jit(solution)/shard_map/while/body/eval_jaxpr/ppermute | solution.py:28
  48.8 0.5 collective-permute-start.2
  49.4 0.8 collective-permute-done.2
  50.8 1.5 fusion.36
  52.2 1.1 copy.47
  53.3 1.1 collective-permute-start
  54.5 3.6 %collective-permute-start.1 = (f32[1,2,40,1,128]{4,2,3,1,0:T(8,128)S(1)}, f32[1,2,40,1,128]{4,2,3,1,0:T(8,128)S(1)}, u32[]{:S(2)}, u32[]{:S(2)}) collective-permute-start(f32[1,2,40,1,128]{4,2,3,1,0:T(8,128)S(1)} %get-tuple-element.103), channel_id=1, source_target_pairs={{2,0},{4,2},{6,4},{8,6},{10,8},{12,10},{14,12},{0,14},{3,1},{5,3},... | collective-permute-start | bytes 122888 | tf_op jit(solution)/shard_map/while/body/eval_jaxpr/ppermute | solution.py:30
  58.1 2.0 %collective-permute-done = f32[1,2,40,1,128]{4,2,3,1,0:T(8,128)S(1)} collective-permute-done((f32[1,2,40,1,128]{4,2,3,1,0:T(8,128)S(1)}, f32[1,2,40,1,128]{4,2,3,1,0:T(8,128)S(1)}, u32[]{:S(2)}, u32[]{:S(2)}) %collective-permute-start) | collective-permute-done | bytes 40992 | tf_op jit(solution)/shard_map/while/body/eval_jaxpr/ppermute | solution.py:28
  61.1 0.5 collective-permute-start.2
  61.7 0.8 collective-permute-done.2
  63.1 1.5 fusion.36
  64.5 1.1 copy.47
  65.7 4.7 %collective-permute-start.1 = (f32[1,2,40,1,128]{4,2,3,1,0:T(8,128)S(1)}, f32[1,2,40,1,128]{4,2,3,1,0:T(8,128)S(1)}, u32[]{:S(2)}, u32[]{:S(2)}) collective-permute-start(f32[1,2,40,1,128]{4,2,3,1,0:T(8,128)S(1)} %get-tuple-element.103), channel_id=1, source_target_pairs={{2,0},{4,2},{6,4},{8,6},{10,8},{12,10},{14,12},{0,14},{3,1},{5,3},... | collective-permute-start | bytes 122888 | tf_op jit(solution)/shard_map/while/body/eval_jaxpr/ppermute | solution.py:30
  70.4 2.0 %collective-permute-done = f32[1,2,40,1,128]{4,2,3,1,0:T(8,128)S(1)} collective-permute-done((f32[1,2,40,1,128]{4,2,3,1,0:T(8,128)S(1)}, f32[1,2,40,1,128]{4,2,3,1,0:T(8,128)S(1)}, u32[]{:S(2)}, u32[]{:S(2)}) %collective-permute-start) | collective-permute-done | bytes 40992 | tf_op jit(solution)/shard_map/while/body/eval_jaxpr/ppermute | solution.py:28
  73.9 0.8 collective-permute-done.2
  75.4 1.5 fusion.36
  76.8 1.1 copy.47
  77.9 4.7 %collective-permute-start.1 = (f32[1,2,40,1,128]{4,2,3,1,0:T(8,128)S(1)}, f32[1,2,40,1,128]{4,2,3,1,0:T(8,128)S(1)}, u32[]{:S(2)}, u32[]{:S(2)}) collective-permute-start(f32[1,2,40,1,128]{4,2,3,1,0:T(8,128)S(1)} %get-tuple-element.103), channel_id=1, source_target_pairs={{2,0},{4,2},{6,4},{8,6},{10,8},{12,10},{14,12},{0,14},{3,1},{5,3},... | collective-permute-start | bytes 122888 | tf_op jit(solution)/shard_map/while/body/eval_jaxpr/ppermute | solution.py:30
  82.6 2.0 %collective-permute-done = f32[1,2,40,1,128]{4,2,3,1,0:T(8,128)S(1)} collective-permute-done((f32[1,2,40,1,128]{4,2,3,1,0:T(8,128)S(1)}, f32[1,2,40,1,128]{4,2,3,1,0:T(8,128)S(1)}, u32[]{:S(2)}, u32[]{:S(2)}) %collective-permute-start) | collective-permute-done | bytes 40992 | tf_op jit(solution)/shard_map/while/body/eval_jaxpr/ppermute | solution.py:28
  86.2 0.8 collective-permute-done.2
  87.7 1.5 fusion.36
  89.1 1.1 copy.47
  90.2 4.7 %collective-permute-start.1 = (f32[1,2,40,1,128]{4,2,3,1,0:T(8,128)S(1)}, f32[1,2,40,1,128]{4,2,3,1,0:T(8,128)S(1)}, u32[]{:S(2)}, u32[]{:S(2)}) collective-permute-start(f32[1,2,40,1,128]{4,2,3,1,0:T(8,128)S(1)} %get-tuple-element.103), channel_id=1, source_target_pairs={{2,0},{4,2},{6,4},{8,6},{10,8},{12,10},{14,12},{0,14},{3,1},{5,3},... | collective-permute-start | bytes 122888 | tf_op jit(solution)/shard_map/while/body/eval_jaxpr/ppermute | solution.py:30
  95.0 2.0 %collective-permute-done = f32[1,2,40,1,128]{4,2,3,1,0:T(8,128)S(1)} collective-permute-done((f32[1,2,40,1,128]{4,2,3,1,0:T(8,128)S(1)}, f32[1,2,40,1,128]{4,2,3,1,0:T(8,128)S(1)}, u32[]{:S(2)}, u32[]{:S(2)}) %collective-permute-start) | collective-permute-done | bytes 40992 | tf_op jit(solution)/shard_map/while/body/eval_jaxpr/ppermute | solution.py:28
  98.5 0.8 collective-permute-done.2
  100.0 1.5 fusion.36
  101.4 1.1 copy.47
  102.5 4.7 %collective-permute-start.1 = (f32[1,2,40,1,128]{4,2,3,1,0:T(8,128)S(1)}, f32[1,2,40,1,128]{4,2,3,1,0:T(8,128)S(1)}, u32[]{:S(2)}, u32[]{:S(2)}) collective-permute-start(f32[1,2,40,1,128]{4,2,3,1,0:T(8,128)S(1)} %get-tuple-element.103), channel_id=1, source_target_pairs={{2,0},{4,2},{6,4},{8,6},{10,8},{12,10},{14,12},{0,14},{3,1},{5,3},... | collective-permute-start | bytes 122888 | tf_op jit(solution)/shard_map/while/body/eval_jaxpr/ppermute | solution.py:30
  107.2 2.0 %collective-permute-done = f32[1,2,40,1,128]{4,2,3,1,0:T(8,128)S(1)} collective-permute-done((f32[1,2,40,1,128]{4,2,3,1,0:T(8,128)S(1)}, f32[1,2,40,1,128]{4,2,3,1,0:T(8,128)S(1)}, u32[]{:S(2)}, u32[]{:S(2)}) %collective-permute-start) | collective-permute-done | bytes 40992 | tf_op jit(solution)/shard_map/while/body/eval_jaxpr/ppermute | solution.py:28
  110.8 0.8 collective-permute-done.2
  112.3 1.5 fusion.36
  113.7 1.1 copy.47
  114.8 4.7 %collective-permute-start.1 = (f32[1,2,40,1,128]{4,2,3,1,0:T(8,128)S(1)}, f32[1,2,40,1,128]{4,2,3,1,0:T(8,128)S(1)}, u32[]{:S(2)}, u32[]{:S(2)}) collective-permute-start(f32[1,2,40,1,128]{4,2,3,1,0:T(8,128)S(1)} %get-tuple-element.103), channel_id=1, source_target_pairs={{2,0},{4,2},{6,4},{8,6},{10,8},{12,10},{14,12},{0,14},{3,1},{5,3},... | collective-permute-start | bytes 122888 | tf_op jit(solution)/shard_map/while/body/eval_jaxpr/ppermute | solution.py:30
  119.5 2.0 %collective-permute-done = f32[1,2,40,1,128]{4,2,3,1,0:T(8,128)S(1)} collective-permute-done((f32[1,2,40,1,128]{4,2,3,1,0:T(8,128)S(1)}, f32[1,2,40,1,128]{4,2,3,1,0:T(8,128)S(1)}, u32[]{:S(2)}, u32[]{:S(2)}) %collective-permute-start) | collective-permute-done | bytes 40992 | tf_op jit(solution)/shard_map/while/body/eval_jaxpr/ppermute | solution.py:28
  123.1 0.8 collective-permute-done.2
  124.5 1.5 fusion.36
  126.0 1.1 copy.47
  127.1 4.7 %collective-permute-start.1 = (f32[1,2,40,1,128]{4,2,3,1,0:T(8,128)S(1)}, f32[1,2,40,1,128]{4,2,3,1,0:T(8,128)S(1)}, u32[]{:S(2)}, u32[]{:S(2)}) collective-permute-start(f32[1,2,40,1,128]{4,2,3,1,0:T(8,128)S(1)} %get-tuple-element.103), channel_id=1, source_target_pairs={{2,0},{4,2},{6,4},{8,6},{10,8},{12,10},{14,12},{0,14},{3,1},{5,3},... | collective-permute-start | bytes 122888 | tf_op jit(solution)/shard_map/while/body/eval_jaxpr/ppermute | solution.py:30
  131.8 2.0 %collective-permute-done = f32[1,2,40,1,128]{4,2,3,1,0:T(8,128)S(1)} collective-permute-done((f32[1,2,40,1,128]{4,2,3,1,0:T(8,128)S(1)}, f32[1,2,40,1,128]{4,2,3,1,0:T(8,128)S(1)}, u32[]{:S(2)}, u32[]{:S(2)}) %collective-permute-start) | collective-permute-done | bytes 40992 | tf_op jit(solution)/shard_map/while/body/eval_jaxpr/ppermute | solution.py:28
  135.4 0.8 collective-permute-done.2
  136.9 1.5 fusion.36
  138.3 1.1 copy.47
  139.4 4.7 %collective-permute-start.1 = (f32[1,2,40,1,128]{4,2,3,1,0:T(8,128)S(1)}, f32[1,2,40,1,128]{4,2,3,1,0:T(8,128)S(1)}, u32[]{:S(2)}, u32[]{:S(2)}) collective-permute-start(f32[1,2,40,1,128]{4,2,3,1,0:T(8,128)S(1)} %get-tuple-element.103), channel_id=1, source_target_pairs={{2,0},{4,2},{6,4},{8,6},{10,8},{12,10},{14,12},{0,14},{3,1},{5,3},... | collective-permute-start | bytes 122888 | tf_op jit(solution)/shard_map/while/body/eval_jaxpr/ppermute | solution.py:30
  144.1 2.0 %collective-permute-done = f32[1,2,40,1,128]{4,2,3,1,0:T(8,128)S(1)} collective-permute-done((f32[1,2,40,1,128]{4,2,3,1,0:T(8,128)S(1)}, f32[1,2,40,1,128]{4,2,3,1,0:T(8,128)S(1)}, u32[]{:S(2)}, u32[]{:S(2)}) %collective-permute-start) | collective-permute-done | bytes 40992 | tf_op jit(solution)/shard_map/while/body/eval_jaxpr/ppermute | solution.py:28
  147.7 0.8 collective-permute-done.2
  149.1 1.5 fusion.36
  150.6 1.1 copy.47
  151.7 4.7 %collective-permute-start.1 = (f32[1,2,40,1,128]{4,2,3,1,0:T(8,128)S(1)}, f32[1,2,40,1,128]{4,2,3,1,0:T(8,128)S(1)}, u32[]{:S(2)}, u32[]{:S(2)}) collective-permute-start(f32[1,2,40,1,128]{4,2,3,1,0:T(8,128)S(1)} %get-tuple-element.103), channel_id=1, source_target_pairs={{2,0},{4,2},{6,4},{8,6},{10,8},{12,10},{14,12},{0,14},{3,1},{5,3},... | collective-permute-start | bytes 122888 | tf_op jit(solution)/shard_map/while/body/eval_jaxpr/ppermute | solution.py:30
  156.4 2.0 %collective-permute-done = f32[1,2,40,1,128]{4,2,3,1,0:T(8,128)S(1)} collective-permute-done((f32[1,2,40,1,128]{4,2,3,1,0:T(8,128)S(1)}, f32[1,2,40,1,128]{4,2,3,1,0:T(8,128)S(1)}, u32[]{:S(2)}, u32[]{:S(2)}) %collective-permute-start) | collective-permute-done | bytes 40992 | tf_op jit(solution)/shard_map/while/body/eval_jaxpr/ppermute | solution.py:28
  160.0 0.8 collective-permute-done.2
  161.4 1.5 fusion.36
  162.9 2.0 %copy.20 = f32[1,2,40,16,128]{4,3,2,1,0:T(8,128)} copy(f32[1,2,40,16,128]{4,2,3,1,0:T(8,128)} %get-tuple-element.32) | data formatting | bytes 1310720 | tf_op jit(solution)/shard_map/while | solution.py:81
  (164 shorter events, 21.9 us)
Async XLA Ops:
  6.5 30.4 %copy-start = (f32[2,80,80]{2,1,0:T(8,128)S(1)}, f32[2,80,80]{2,1,0:T(8,128)}, u32[]{:S(2)}) copy-start(f32[2,80,80]{2,1,0:T(8,128)} %param.8) | copy-start | bytes 153604
  6.5 30.4 %all-gather.2.cloned.1.call-start = ((), (), s32[]{:S(2)}) async-start(), calls=%async_computation | async-start | bytes 1966080 | tf_op jit(solution)/shard_map/all_gather | solution.py:59
  7.7 2.2 %copy-start.1 = (f32[2,16,128]{2,1,0:T(8,128)S(1)}, f32[2,16,128]{2,1,0:T(8,128)}, u32[]{:S(2)}) copy-start(f32[2,16,128]{2,1,0:T(8,128)} %param.9) | copy-start | bytes 49156
  9.9 7.6 %collective-permute-start.4 = (f32[1,128]{1,0:T(1,128)S(1)}, f32[1,128]{1,0:T(1,128)S(1)}, u32[]{:S(2)}, u32[]{:S(2)}) collective-permute-start(f32[1,128]{1,0:T(1,128)S(1)} %slice_bitcast_fusion.1), channel_id=1, source_target_pairs={{14,0},{0,2},{2,4},{4,6},{6,8},{8,10},{10,12},{12,14},{15,1},{1,3}... | collective-permute-start | bytes 1544 | tf_op jit(solution)/shard_map/ppermute | solution.py:12
  13.0 2.3 %collective-permute-start.5 = (f32[16,1]{1,0:T(8,128)S(1)}, f32[16,1]{1,0:T(8,128)S(1)}, u32[]{:S(2)}, u32[]{:S(2)}) collective-permute-start(f32[16,1]{1,0:T(8,128)S(1)} %slice.63), channel_id=1, source_target_pairs={{0,1},{2,3},{4,5},{6,7},{8,9},{10,11},{12,13},{14,15},{16,17},{18,... | collective-permute-start | bytes 200 | tf_op jit(solution)/shard_map/ppermute | solution.py:18
  41.1 6.7 %collective-permute-start = (f32[1,2,40,1,128]{4,2,3,1,0:T(8,128)S(1)}, f32[1,2,40,1,128]{4,2,3,1,0:T(8,128)S(1)}, u32[]{:S(2)}, u32[]{:S(2)}) collective-permute-start(f32[1,2,40,1,128]{4,2,3,1,0:T(8,128)S(1)} %get-tuple-element.102), channel_id=1, source_target_pairs={{0,2},{2,4},{4,6},{6,8},{8,10},{10,12},{12,14},{14,0},{1,3},{3,5},... | collective-permute-start | bytes 122888 | tf_op jit(solution)/shard_map/while/body/eval_jaxpr/ppermute | solution.py:28
  42.6 5.2 %collective-permute-start.1 = (f32[1,2,40,1,128]{4,2,3,1,0:T(8,128)S(1)}, f32[1,2,40,1,128]{4,2,3,1,0:T(8,128)S(1)}, u32[]{:S(2)}, u32[]{:S(2)}) collective-permute-start(f32[1,2,40,1,128]{4,2,3,1,0:T(8,128)S(1)} %get-tuple-element.103), channel_id=1, source_target_pairs={{2,0},{4,2},{6,4},{8,6},{10,8},{12,10},{14,12},{0,14},{3,1},{5,3},... | collective-permute-start | bytes 122888 | tf_op jit(solution)/shard_map/while/body/eval_jaxpr/ppermute | solution.py:30
  48.7 1.8 %collective-permute-start.3 = (f32[1,2,40,18,1]{2,1,4,3,0:T(2,128)S(1)}, f32[1,2,40,18,1]{2,1,4,3,0:T(2,128)S(1)}, u32[]{:S(2)}, u32[]{:S(2)}) collective-permute-start(f32[1,2,40,18,1]{2,1,4,3,0:T(2,128)S(1)} %copy.34), channel_id=1, source_target_pairs={{1,0},{0,1},{3,2},{2,3},{5,4},{4,5},{7,6},{6,7},{9,8},{8,9},{11,10... | collective-permute-start | bytes 17288 | tf_op jit(solution)/shard_map/while/body/eval_jaxpr/ppermute | solution.py:30
  48.8 1.3 collective-permute-start.2
  53.3 6.7 %collective-permute-start = (f32[1,2,40,1,128]{4,2,3,1,0:T(8,128)S(1)}, f32[1,2,40,1,128]{4,2,3,1,0:T(8,128)S(1)}, u32[]{:S(2)}, u32[]{:S(2)}) collective-permute-start(f32[1,2,40,1,128]{4,2,3,1,0:T(8,128)S(1)} %get-tuple-element.102), channel_id=1, source_target_pairs={{0,2},{2,4},{4,6},{6,8},{8,10},{10,12},{12,14},{14,0},{1,3},{3,5},... | collective-permute-start | bytes 122888 | tf_op jit(solution)/shard_map/while/body/eval_jaxpr/ppermute | solution.py:28
  54.5 5.7 %collective-permute-start.1 = (f32[1,2,40,1,128]{4,2,3,1,0:T(8,128)S(1)}, f32[1,2,40,1,128]{4,2,3,1,0:T(8,128)S(1)}, u32[]{:S(2)}, u32[]{:S(2)}) collective-permute-start(f32[1,2,40,1,128]{4,2,3,1,0:T(8,128)S(1)} %get-tuple-element.103), channel_id=1, source_target_pairs={{2,0},{4,2},{6,4},{8,6},{10,8},{12,10},{14,12},{0,14},{3,1},{5,3},... | collective-permute-start | bytes 122888 | tf_op jit(solution)/shard_map/while/body/eval_jaxpr/ppermute | solution.py:30
  61.0 1.8 %collective-permute-start.3 = (f32[1,2,40,18,1]{2,1,4,3,0:T(2,128)S(1)}, f32[1,2,40,18,1]{2,1,4,3,0:T(2,128)S(1)}, u32[]{:S(2)}, u32[]{:S(2)}) collective-permute-start(f32[1,2,40,18,1]{2,1,4,3,0:T(2,128)S(1)} %copy.34), channel_id=1, source_target_pairs={{1,0},{0,1},{3,2},{2,3},{5,4},{4,5},{7,6},{6,7},{9,8},{8,9},{11,10... | collective-permute-start | bytes 17288 | tf_op jit(solution)/shard_map/while/body/eval_jaxpr/ppermute | solution.py:30
  61.1 1.3 collective-permute-start.2
  65.6 6.7 %collective-permute-start = (f32[1,2,40,1,128]{4,2,3,1,0:T(8,128)S(1)}, f32[1,2,40,1,128]{4,2,3,1,0:T(8,128)S(1)}, u32[]{:S(2)}, u32[]{:S(2)}) collective-permute-start(f32[1,2,40,1,128]{4,2,3,1,0:T(8,128)S(1)} %get-tuple-element.102), channel_id=1, source_target_pairs={{0,2},{2,4},{4,6},{6,8},{8,10},{10,12},{12,14},{14,0},{1,3},{3,5},... | collective-permute-start | bytes 122888 | tf_op jit(solution)/shard_map/while/body/eval_jaxpr/ppermute | solution.py:28
  65.7 6.7 %collective-permute-start.1 = (f32[1,2,40,1,128]{4,2,3,1,0:T(8,128)S(1)}, f32[1,2,40,1,128]{4,2,3,1,0:T(8,128)S(1)}, u32[]{:S(2)}, u32[]{:S(2)}) collective-permute-start(f32[1,2,40,1,128]{4,2,3,1,0:T(8,128)S(1)} %get-tuple-element.103), channel_id=1, source_target_pairs={{2,0},{4,2},{6,4},{8,6},{10,8},{12,10},{14,12},{0,14},{3,1},{5,3},... | collective-permute-start | bytes 122888 | tf_op jit(solution)/shard_map/while/body/eval_jaxpr/ppermute | solution.py:30
  73.3 1.8 %collective-permute-start.3 = (f32[1,2,40,18,1]{2,1,4,3,0:T(2,128)S(1)}, f32[1,2,40,18,1]{2,1,4,3,0:T(2,128)S(1)}, u32[]{:S(2)}, u32[]{:S(2)}) collective-permute-start(f32[1,2,40,18,1]{2,1,4,3,0:T(2,128)S(1)} %copy.34), channel_id=1, source_target_pairs={{1,0},{0,1},{3,2},{2,3},{5,4},{4,5},{7,6},{6,7},{9,8},{8,9},{11,10... | collective-permute-start | bytes 17288 | tf_op jit(solution)/shard_map/while/body/eval_jaxpr/ppermute | solution.py:30
  73.4 1.3 collective-permute-start.2
  77.9 6.7 %collective-permute-start = (f32[1,2,40,1,128]{4,2,3,1,0:T(8,128)S(1)}, f32[1,2,40,1,128]{4,2,3,1,0:T(8,128)S(1)}, u32[]{:S(2)}, u32[]{:S(2)}) collective-permute-start(f32[1,2,40,1,128]{4,2,3,1,0:T(8,128)S(1)} %get-tuple-element.102), channel_id=1, source_target_pairs={{0,2},{2,4},{4,6},{6,8},{8,10},{10,12},{12,14},{14,0},{1,3},{3,5},... | collective-permute-start | bytes 122888 | tf_op jit(solution)/shard_map/while/body/eval_jaxpr/ppermute | solution.py:28
  77.9 6.8 %collective-permute-start.1 = (f32[1,2,40,1,128]{4,2,3,1,0:T(8,128)S(1)}, f32[1,2,40,1,128]{4,2,3,1,0:T(8,128)S(1)}, u32[]{:S(2)}, u32[]{:S(2)}) collective-permute-start(f32[1,2,40,1,128]{4,2,3,1,0:T(8,128)S(1)} %get-tuple-element.103), channel_id=1, source_target_pairs={{2,0},{4,2},{6,4},{8,6},{10,8},{12,10},{14,12},{0,14},{3,1},{5,3},... | collective-permute-start | bytes 122888 | tf_op jit(solution)/shard_map/while/body/eval_jaxpr/ppermute | solution.py:30
  85.6 1.8 %collective-permute-start.3 = (f32[1,2,40,18,1]{2,1,4,3,0:T(2,128)S(1)}, f32[1,2,40,18,1]{2,1,4,3,0:T(2,128)S(1)}, u32[]{:S(2)}, u32[]{:S(2)}) collective-permute-start(f32[1,2,40,18,1]{2,1,4,3,0:T(2,128)S(1)} %copy.34), channel_id=1, source_target_pairs={{1,0},{0,1},{3,2},{2,3},{5,4},{4,5},{7,6},{6,7},{9,8},{8,9},{11,10... | collective-permute-start | bytes 17288 | tf_op jit(solution)/shard_map/while/body/eval_jaxpr/ppermute | solution.py:30
  85.7 1.3 collective-permute-start.2
  90.2 6.7 %collective-permute-start = (f32[1,2,40,1,128]{4,2,3,1,0:T(8,128)S(1)}, f32[1,2,40,1,128]{4,2,3,1,0:T(8,128)S(1)}, u32[]{:S(2)}, u32[]{:S(2)}) collective-permute-start(f32[1,2,40,1,128]{4,2,3,1,0:T(8,128)S(1)} %get-tuple-element.102), channel_id=1, source_target_pairs={{0,2},{2,4},{4,6},{6,8},{8,10},{10,12},{12,14},{14,0},{1,3},{3,5},... | collective-permute-start | bytes 122888 | tf_op jit(solution)/shard_map/while/body/eval_jaxpr/ppermute | solution.py:28
  90.2 6.7 %collective-permute-start.1 = (f32[1,2,40,1,128]{4,2,3,1,0:T(8,128)S(1)}, f32[1,2,40,1,128]{4,2,3,1,0:T(8,128)S(1)}, u32[]{:S(2)}, u32[]{:S(2)}) collective-permute-start(f32[1,2,40,1,128]{4,2,3,1,0:T(8,128)S(1)} %get-tuple-element.103), channel_id=1, source_target_pairs={{2,0},{4,2},{6,4},{8,6},{10,8},{12,10},{14,12},{0,14},{3,1},{5,3},... | collective-permute-start | bytes 122888 | tf_op jit(solution)/shard_map/while/body/eval_jaxpr/ppermute | solution.py:30
  97.9 1.8 %collective-permute-start.3 = (f32[1,2,40,18,1]{2,1,4,3,0:T(2,128)S(1)}, f32[1,2,40,18,1]{2,1,4,3,0:T(2,128)S(1)}, u32[]{:S(2)}, u32[]{:S(2)}) collective-permute-start(f32[1,2,40,18,1]{2,1,4,3,0:T(2,128)S(1)} %copy.34), channel_id=1, source_target_pairs={{1,0},{0,1},{3,2},{2,3},{5,4},{4,5},{7,6},{6,7},{9,8},{8,9},{11,10... | collective-permute-start | bytes 17288 | tf_op jit(solution)/shard_map/while/body/eval_jaxpr/ppermute | solution.py:30
  98.0 1.3 collective-permute-start.2
  102.5 6.7 %collective-permute-start = (f32[1,2,40,1,128]{4,2,3,1,0:T(8,128)S(1)}, f32[1,2,40,1,128]{4,2,3,1,0:T(8,128)S(1)}, u32[]{:S(2)}, u32[]{:S(2)}) collective-permute-start(f32[1,2,40,1,128]{4,2,3,1,0:T(8,128)S(1)} %get-tuple-element.102), channel_id=1, source_target_pairs={{0,2},{2,4},{4,6},{6,8},{8,10},{10,12},{12,14},{14,0},{1,3},{3,5},... | collective-permute-start | bytes 122888 | tf_op jit(solution)/shard_map/while/body/eval_jaxpr/ppermute | solution.py:28
  102.5 6.8 %collective-permute-start.1 = (f32[1,2,40,1,128]{4,2,3,1,0:T(8,128)S(1)}, f32[1,2,40,1,128]{4,2,3,1,0:T(8,128)S(1)}, u32[]{:S(2)}, u32[]{:S(2)}) collective-permute-start(f32[1,2,40,1,128]{4,2,3,1,0:T(8,128)S(1)} %get-tuple-element.103), channel_id=1, source_target_pairs={{2,0},{4,2},{6,4},{8,6},{10,8},{12,10},{14,12},{0,14},{3,1},{5,3},... | collective-permute-start | bytes 122888 | tf_op jit(solution)/shard_map/while/body/eval_jaxpr/ppermute | solution.py:30
  110.2 1.8 %collective-permute-start.3 = (f32[1,2,40,18,1]{2,1,4,3,0:T(2,128)S(1)}, f32[1,2,40,18,1]{2,1,4,3,0:T(2,128)S(1)}, u32[]{:S(2)}, u32[]{:S(2)}) collective-permute-start(f32[1,2,40,18,1]{2,1,4,3,0:T(2,128)S(1)} %copy.34), channel_id=1, source_target_pairs={{1,0},{0,1},{3,2},{2,3},{5,4},{4,5},{7,6},{6,7},{9,8},{8,9},{11,10... | collective-permute-start | bytes 17288 | tf_op jit(solution)/shard_map/while/body/eval_jaxpr/ppermute | solution.py:30
  110.3 1.3 collective-permute-start.2
  114.8 6.7 %collective-permute-start = (f32[1,2,40,1,128]{4,2,3,1,0:T(8,128)S(1)}, f32[1,2,40,1,128]{4,2,3,1,0:T(8,128)S(1)}, u32[]{:S(2)}, u32[]{:S(2)}) collective-permute-start(f32[1,2,40,1,128]{4,2,3,1,0:T(8,128)S(1)} %get-tuple-element.102), channel_id=1, source_target_pairs={{0,2},{2,4},{4,6},{6,8},{8,10},{10,12},{12,14},{14,0},{1,3},{3,5},... | collective-permute-start | bytes 122888 | tf_op jit(solution)/shard_map/while/body/eval_jaxpr/ppermute | solution.py:28
  114.8 6.7 %collective-permute-start.1 = (f32[1,2,40,1,128]{4,2,3,1,0:T(8,128)S(1)}, f32[1,2,40,1,128]{4,2,3,1,0:T(8,128)S(1)}, u32[]{:S(2)}, u32[]{:S(2)}) collective-permute-start(f32[1,2,40,1,128]{4,2,3,1,0:T(8,128)S(1)} %get-tuple-element.103), channel_id=1, source_target_pairs={{2,0},{4,2},{6,4},{8,6},{10,8},{12,10},{14,12},{0,14},{3,1},{5,3},... | collective-permute-start | bytes 122888 | tf_op jit(solution)/shard_map/while/body/eval_jaxpr/ppermute | solution.py:30
  122.5 1.8 %collective-permute-start.3 = (f32[1,2,40,18,1]{2,1,4,3,0:T(2,128)S(1)}, f32[1,2,40,18,1]{2,1,4,3,0:T(2,128)S(1)}, u32[]{:S(2)}, u32[]{:S(2)}) collective-permute-start(f32[1,2,40,18,1]{2,1,4,3,0:T(2,128)S(1)} %copy.34), channel_id=1, source_target_pairs={{1,0},{0,1},{3,2},{2,3},{5,4},{4,5},{7,6},{6,7},{9,8},{8,9},{11,10... | collective-permute-start | bytes 17288 | tf_op jit(solution)/shard_map/while/body/eval_jaxpr/ppermute | solution.py:30
  122.5 1.3 collective-permute-start.2
  127.1 6.7 %collective-permute-start = (f32[1,2,40,1,128]{4,2,3,1,0:T(8,128)S(1)}, f32[1,2,40,1,128]{4,2,3,1,0:T(8,128)S(1)}, u32[]{:S(2)}, u32[]{:S(2)}) collective-permute-start(f32[1,2,40,1,128]{4,2,3,1,0:T(8,128)S(1)} %get-tuple-element.102), channel_id=1, source_target_pairs={{0,2},{2,4},{4,6},{6,8},{8,10},{10,12},{12,14},{14,0},{1,3},{3,5},... | collective-permute-start | bytes 122888 | tf_op jit(solution)/shard_map/while/body/eval_jaxpr/ppermute | solution.py:28
  127.1 6.8 %collective-permute-start.1 = (f32[1,2,40,1,128]{4,2,3,1,0:T(8,128)S(1)}, f32[1,2,40,1,128]{4,2,3,1,0:T(8,128)S(1)}, u32[]{:S(2)}, u32[]{:S(2)}) collective-permute-start(f32[1,2,40,1,128]{4,2,3,1,0:T(8,128)S(1)} %get-tuple-element.103), channel_id=1, source_target_pairs={{2,0},{4,2},{6,4},{8,6},{10,8},{12,10},{14,12},{0,14},{3,1},{5,3},... | collective-permute-start | bytes 122888 | tf_op jit(solution)/shard_map/while/body/eval_jaxpr/ppermute | solution.py:30
  134.8 1.8 %collective-permute-start.3 = (f32[1,2,40,18,1]{2,1,4,3,0:T(2,128)S(1)}, f32[1,2,40,18,1]{2,1,4,3,0:T(2,128)S(1)}, u32[]{:S(2)}, u32[]{:S(2)}) collective-permute-start(f32[1,2,40,18,1]{2,1,4,3,0:T(2,128)S(1)} %copy.34), channel_id=1, source_target_pairs={{1,0},{0,1},{3,2},{2,3},{5,4},{4,5},{7,6},{6,7},{9,8},{8,9},{11,10... | collective-permute-start | bytes 17288 | tf_op jit(solution)/shard_map/while/body/eval_jaxpr/ppermute | solution.py:30
  134.8 1.3 collective-permute-start.2
  139.4 6.7 %collective-permute-start = (f32[1,2,40,1,128]{4,2,3,1,0:T(8,128)S(1)}, f32[1,2,40,1,128]{4,2,3,1,0:T(8,128)S(1)}, u32[]{:S(2)}, u32[]{:S(2)}) collective-permute-start(f32[1,2,40,1,128]{4,2,3,1,0:T(8,128)S(1)} %get-tuple-element.102), channel_id=1, source_target_pairs={{0,2},{2,4},{4,6},{6,8},{8,10},{10,12},{12,14},{14,0},{1,3},{3,5},... | collective-permute-start | bytes 122888 | tf_op jit(solution)/shard_map/while/body/eval_jaxpr/ppermute | solution.py:28
  139.4 6.7 %collective-permute-start.1 = (f32[1,2,40,1,128]{4,2,3,1,0:T(8,128)S(1)}, f32[1,2,40,1,128]{4,2,3,1,0:T(8,128)S(1)}, u32[]{:S(2)}, u32[]{:S(2)}) collective-permute-start(f32[1,2,40,1,128]{4,2,3,1,0:T(8,128)S(1)} %get-tuple-element.103), channel_id=1, source_target_pairs={{2,0},{4,2},{6,4},{8,6},{10,8},{12,10},{14,12},{0,14},{3,1},{5,3},... | collective-permute-start | bytes 122888 | tf_op jit(solution)/shard_map/while/body/eval_jaxpr/ppermute | solution.py:30
  147.0 1.8 %collective-permute-start.3 = (f32[1,2,40,18,1]{2,1,4,3,0:T(2,128)S(1)}, f32[1,2,40,18,1]{2,1,4,3,0:T(2,128)S(1)}, u32[]{:S(2)}, u32[]{:S(2)}) collective-permute-start(f32[1,2,40,18,1]{2,1,4,3,0:T(2,128)S(1)} %copy.34), channel_id=1, source_target_pairs={{1,0},{0,1},{3,2},{2,3},{5,4},{4,5},{7,6},{6,7},{9,8},{8,9},{11,10... | collective-permute-start | bytes 17288 | tf_op jit(solution)/shard_map/while/body/eval_jaxpr/ppermute | solution.py:30
  147.1 1.3 collective-permute-start.2
  151.7 6.7 %collective-permute-start = (f32[1,2,40,1,128]{4,2,3,1,0:T(8,128)S(1)}, f32[1,2,40,1,128]{4,2,3,1,0:T(8,128)S(1)}, u32[]{:S(2)}, u32[]{:S(2)}) collective-permute-start(f32[1,2,40,1,128]{4,2,3,1,0:T(8,128)S(1)} %get-tuple-element.102), channel_id=1, source_target_pairs={{0,2},{2,4},{4,6},{6,8},{8,10},{10,12},{12,14},{14,0},{1,3},{3,5},... | collective-permute-start | bytes 122888 | tf_op jit(solution)/shard_map/while/body/eval_jaxpr/ppermute | solution.py:28
  151.7 6.8 %collective-permute-start.1 = (f32[1,2,40,1,128]{4,2,3,1,0:T(8,128)S(1)}, f32[1,2,40,1,128]{4,2,3,1,0:T(8,128)S(1)}, u32[]{:S(2)}, u32[]{:S(2)}) collective-permute-start(f32[1,2,40,1,128]{4,2,3,1,0:T(8,128)S(1)} %get-tuple-element.103), channel_id=1, source_target_pairs={{2,0},{4,2},{6,4},{8,6},{10,8},{12,10},{14,12},{0,14},{3,1},{5,3},... | collective-permute-start | bytes 122888 | tf_op jit(solution)/shard_map/while/body/eval_jaxpr/ppermute | solution.py:30
  159.4 1.8 %collective-permute-start.3 = (f32[1,2,40,18,1]{2,1,4,3,0:T(2,128)S(1)}, f32[1,2,40,18,1]{2,1,4,3,0:T(2,128)S(1)}, u32[]{:S(2)}, u32[]{:S(2)}) collective-permute-start(f32[1,2,40,18,1]{2,1,4,3,0:T(2,128)S(1)} %copy.34), channel_id=1, source_target_pairs={{1,0},{0,1},{3,2},{2,3},{5,4},{4,5},{7,6},{6,7},{9,8},{8,9},{11,10... | collective-permute-start | bytes 17288 | tf_op jit(solution)/shard_map/while/body/eval_jaxpr/ppermute | solution.py:30
  159.4 1.3 collective-permute-start.2
Sparse Core Ops, SparseCore 0:
  10.0 26.9 all-gather.1
where the time goes:
time: 172 us
  starting transfers between devices  57.3 us (33%)
  waiting for transfers between devices  49.7 us (29%)
  local copies, waits for them, and re-layouts  29.9 us (17%)
  other arithmetic  17.9 us (10%)
  between operations  13.4 us (8%)
  matrix products  3.01 us (2%)
    ppermute x20, starting transfers between devices, padded(): lax.ppermute(head, axis, [((i + 1) % count, i) for i in range(count)])  45.2 us
    ppermute x20, waiting for transfers between devices, padded(): lax.ppermute(tail, axis, [(i, (i + 1) % count) for i in range(count)])  27.5 us
    all_gather x1, waiting for transfers between devices, per_device(): lax.all_gather(masked, 'lev', axis=2, tiled=True)  19.4 us
    while x50, local copies, waits for them, and re-layouts  17.4 us
    mul x10, other arithmetic, relax(): return wet_center * (center + flux)  14.5 us
    ppermute x20, starting transfers between devices, padded(): lax.ppermute(tail, axis, [(i, (i + 1) % count) for i in range(count)])  7.65 us
  transfers between devices with their start and end apart: 43, of which 23 were waited for; matrix products, arithmetic and copies ran while one was open for 3% of the time, Pallas kernels for 0%

commit v1 on v0

--- a/solution.py
+++ b/solution.py
@@ -2,6 +2,7 @@
 import jax.numpy as jnp
 from jax import lax
 from jax.sharding import PartitionSpec as P
+from jax.lax import axis_index, axis_size, ppermute
 
 PASSES = 10
 
@@ -44,6 +45,23 @@
 
 
 def per_device(increments, vert_corr, kappa, sea_mask, level_count):
+
+    def bind_the_fields(xs, mesh_name):
+        arr_out = axis_index(mesh_name)
+        far_arr = axis_size(mesh_name)
+        v_next, piece_out = (far_arr, arr_out)
+        plain, w_next = (xs, 1)
+        while w_next < v_next:
+            seen = []
+            for no in [*range(v_next)]:
+                seen.append((no, no ^ w_next))
+            block_now = ppermute(plain, mesh_name, seen)
+            placed = jnp.concatenate([plain, block_now], 2)
+            reply = jnp.concatenate([block_now, plain], 2)
+            plain = jnp.where(piece_out & w_next == 0, placed, reply)
+            w_next = 2 * w_next
+        return plain
+
     lev_dev = sea_mask.shape[0]
     cells_x = sea_mask.shape[1]
     cells_y = sea_mask.shape[2]
@@ -56,7 +74,7 @@
     correlated = jnp.einsum(
         "toh,dthxy->dtoxy",
         own_rows,
-        lax.all_gather(masked, "lev", axis=2, tiled=True),
+        bind_the_fields(masked, mesh_name="lev"),
         precision=lax.Precision.HIGHEST,
     )
     field = correlated * wet_float

time: 172 us -> 151 us (0.88)
  between operations: 13.4 us -> 0.07 us
  waiting for transfers between devices: 49.7 us -> 41 us
    all_gather x1 -> x0, waiting for transfers between devices: 19.4 us -> none  [per_device(): lax.all_gather(masked, 'lev', axis=2, tiled=True)]
    ppermute x0 -> x1, waiting for transfers between devices: none -> 13.4 us  [bind_the_fields(): block_now = ppermute(plain, mesh_name, seen)]
    ppermute x1, waiting for transfers between devices: 2.12 us -> 0.01 us  [from_behind(): return lax.ppermute(block, axis, route)]
    mul x1, other arithmetic: 2.14 us -> 0.21 us  [per_device(): masked = increments * wet_float]
  transfers between devices with their start and end apart: 43 -> 43, of which waited for: 23 -> 21; matrix products, arithmetic and copies ran while one was open for 3% -> 5% of each run, Pallas kernels for 0% -> 0%
where the time goes in v1:
time: 151 us; the launch traced here: 150 us
  starting transfers between devices  58.8 us (39%)
  waiting for transfers between devices  41 us (27%)
  local copies, waits for them, and re-layouts  31.1 us (21%)
  other arithmetic  16.8 us (11%)
  matrix products  1.77 us (1%)
    ppermute x20, starting transfers between devices, padded(): lax.ppermute(head, axis, [((i + 1) % count, i) for i in range(count)])  45.2 us
    ppermute x20, waiting for transfers between devices, padded(): lax.ppermute(tail, axis, [(i, (i + 1) % count) for i in range(count)])  27.5 us
    while x50, local copies, waits for them, and re-layouts  17.4 us
    mul x10, other arithmetic, relax(): return wet_center * (center + flux)  14.4 us
    ppermute x1, waiting for transfers between devices, bind_the_fields(): block_now = ppermute(plain, mesh_name, seen)  13.4 us
    ppermute x20, starting transfers between devices, padded(): lax.ppermute(tail, axis, [(i, (i + 1) % count) for i in range(count)])  7.68 us
    ppermute x10, local copies, waits for them, and re-layouts, padded(): lax.ppermute(head, axis, [((i + 1) % count, i) for i in range(count)])  3.31 us
    ppermute x10, local copies, waits for them, and re-layouts, padded(): lax.ppermute(tail, axis, [(i, (i + 1) % count) for i in range(count)])  3.3 us
  transfers between devices with their start and end apart: 43, of which 21 were waited for; matrix products, arithmetic and copies ran while one was open for 5% of the time, Pallas kernels for 0%

profile of v1, /device:TPU:0, one launch (start us, length us, event | category | flops | bytes accessed | tf_op | source)
XLA Modules:
  0.0 150.1 jit_solution(8482062386391403629)
XLA Ops:
  0.0 0.8 slice_bitcast_fusion.1
  0.8 3.0 %collective-permute-start.5 = (f32[1,128]{1,0:T(1,128)S(1)}, f32[1,128]{1,0:T(1,128)S(1)}, u32[]{:S(2)}, u32[]{:S(2)}) collective-permute-start(f32[1,128]{1,0:T(1,128)S(1)} %slice_bitcast_fusion.1), channel_id=1, source_target_pairs={{14,0},{0,2},{2,4},{4,6},{6,8},{8,10},{10,12},{12,14},{15,1},{1,3}... | collective-permute-start | bytes 1544 | tf_op jit(solution)/shard_map/ppermute | solution.py:13
  3.7 0.7 bitcast_multiply_fusion
  4.5 1.4 collective-permute-start.6
  6.0 1.1 fusion.22
  7.3 1.6 %collective-permute-start.4 = (f32[1,2,40,16,128]{4,2,3,1,0:T(8,128)S(1)}, f32[1,2,40,16,128]{4,2,3,1,0:T(8,128)S(1)}, u32[]{:S(2)}, u32[]{:S(2)}) collective-permute-start(f32[1,2,40,16,128]{4,2,3,1,0:T(8,128)S(1)} %copy_multiply_fusion), channel_id=1, source_target_pairs={{0,16},{16,0},{1,17},{17,1},{2,18},{18,2},{3,19},{19,3},{4,20},{20... | collective-permute-start | bytes 1966088 | tf_op jit(solution)/shard_map/ppermute | solution.py:58
  10.0 13.4 %collective-permute-done.4 = f32[1,2,40,16,128]{4,2,3,1,0:T(8,128)S(1)} collective-permute-done((f32[1,2,40,16,128]{4,2,3,1,0:T(8,128)S(1)}, f32[1,2,40,16,128]{4,2,3,1,0:T(8,128)S(1)}, u32[]{:S(2)}, u32[]{:S(2)}) %collective-permute-start.4) | collective-permute-done | bytes 655392 | tf_op jit(solution)/shard_map/ppermute | solution.py:58
  23.4 1.8 %fusion.20 = f32[1,2,40,16,128]{4,2,3,1,0:T(8,128)} fusion(f32[2,40,16,128]{3,1,2,0:T(8,128)S(1)} %bitcast.22, f32[2,40,16,128]{3,1,2,0:T(8,128)S(1)} %fusion.31, pred[]{:T(512)S(6)} %eq.3, f32[40,16,128]{2,0,1:T(8,128)S(1)} %fusion.22, f32[2,80,80]{2,1,0:T(8,128)S(1)} %copy-done, s32[]{:T(128)S(6)} %select_n.16), kind=kOutput, calls=%fused_computation.28 | convolution fusion | flops 158433280 | bytes 2334725 | tf_op jit(solution)/shard_map/toh,dthxy->dtoxy/dot_general | solution.py:74
  25.2 122.9 %while.10 = (s32[]{:T(128)}, f32[1,2,40,16,128]{4,2,3,1,0:T(8,128)}, f32[40,16,128]{2,0,1:T(8,128)S(1)}, f32[18,130]{1,0:T(8,128)S(1)}, f32[18,130]{1,0:T(8,128)S(1)}, /*index=5*/s32[]{:T(128)}) while((s32[]{:T(128)}, f32[1,2,40,16,128]{4,2,3,1,0:T(8,128)}, f32[40,16,128]{2,0,1:T(8,128)S(1)}, f32[18,130]{1,0:T(8,128)S(1)}, ...), condition=%wide.region_1.2_spmd, body=%wide.region_0.1_spmd.sunk | while | flops 2785282 | bytes 5959653 | solution.py:99
  25.2 1.1 copy.49
  26.3 1.5 %collective-permute-start = (f32[1,2,40,1,128]{4,2,3,1,0:T(8,128)S(1)}, f32[1,2,40,1,128]{4,2,3,1,0:T(8,128)S(1)}, u32[]{:S(2)}, u32[]{:S(2)}) collective-permute-start(f32[1,2,40,1,128]{4,2,3,1,0:T(8,128)S(1)} %get-tuple-element.102), channel_id=1, source_target_pairs={{0,2},{2,4},{4,6},{6,8},{8,10},{10,12},{12,14},{14,0},{1,3},{3,5},... | collective-permute-start | bytes 122888 | tf_op jit(solution)/shard_map/while/body/eval_jaxpr/ppermute | solution.py:29
  27.8 3.2 %collective-permute-start.1 = (f32[1,2,40,1,128]{4,2,3,1,0:T(8,128)S(1)}, f32[1,2,40,1,128]{4,2,3,1,0:T(8,128)S(1)}, u32[]{:S(2)}, u32[]{:S(2)}) collective-permute-start(f32[1,2,40,1,128]{4,2,3,1,0:T(8,128)S(1)} %get-tuple-element.103), channel_id=1, source_target_pairs={{2,0},{4,2},{6,4},{8,6},{10,8},{12,10},{14,12},{0,14},{3,1},{5,3},... | collective-permute-start | bytes 122888 | tf_op jit(solution)/shard_map/while/body/eval_jaxpr/ppermute | solution.py:31
  31.0 2.0 %collective-permute-done = f32[1,2,40,1,128]{4,2,3,1,0:T(8,128)S(1)} collective-permute-done((f32[1,2,40,1,128]{4,2,3,1,0:T(8,128)S(1)}, f32[1,2,40,1,128]{4,2,3,1,0:T(8,128)S(1)}, u32[]{:S(2)}, u32[]{:S(2)}) %collective-permute-start) | collective-permute-done | bytes 40992 | tf_op jit(solution)/shard_map/while/body/eval_jaxpr/ppermute | solution.py:29
  34.0 0.5 collective-permute-start.2
  34.6 0.8 collective-permute-done.2
  36.0 1.4 fusion.39
  37.4 1.1 copy.49
  38.5 1.2 collective-permute-start
  39.7 3.6 %collective-permute-start.1 = (f32[1,2,40,1,128]{4,2,3,1,0:T(8,128)S(1)}, f32[1,2,40,1,128]{4,2,3,1,0:T(8,128)S(1)}, u32[]{:S(2)}, u32[]{:S(2)}) collective-permute-start(f32[1,2,40,1,128]{4,2,3,1,0:T(8,128)S(1)} %get-tuple-element.103), channel_id=1, source_target_pairs={{2,0},{4,2},{6,4},{8,6},{10,8},{12,10},{14,12},{0,14},{3,1},{5,3},... | collective-permute-start | bytes 122888 | tf_op jit(solution)/shard_map/while/body/eval_jaxpr/ppermute | solution.py:31
  43.3 2.0 %collective-permute-done = f32[1,2,40,1,128]{4,2,3,1,0:T(8,128)S(1)} collective-permute-done((f32[1,2,40,1,128]{4,2,3,1,0:T(8,128)S(1)}, f32[1,2,40,1,128]{4,2,3,1,0:T(8,128)S(1)}, u32[]{:S(2)}, u32[]{:S(2)}) %collective-permute-start) | collective-permute-done | bytes 40992 | tf_op jit(solution)/shard_map/while/body/eval_jaxpr/ppermute | solution.py:29
  46.3 0.5 collective-permute-start.2
  46.9 0.8 collective-permute-done.2
  48.3 1.4 fusion.39
  49.7 1.1 copy.49
  50.8 4.7 %collective-permute-start.1 = (f32[1,2,40,1,128]{4,2,3,1,0:T(8,128)S(1)}, f32[1,2,40,1,128]{4,2,3,1,0:T(8,128)S(1)}, u32[]{:S(2)}, u32[]{:S(2)}) collective-permute-start(f32[1,2,40,1,128]{4,2,3,1,0:T(8,128)S(1)} %get-tuple-element.103), channel_id=1, source_target_pairs={{2,0},{4,2},{6,4},{8,6},{10,8},{12,10},{14,12},{0,14},{3,1},{5,3},... | collective-permute-start | bytes 122888 | tf_op jit(solution)/shard_map/while/body/eval_jaxpr/ppermute | solution.py:31
  55.6 2.0 %collective-permute-done = f32[1,2,40,1,128]{4,2,3,1,0:T(8,128)S(1)} collective-permute-done((f32[1,2,40,1,128]{4,2,3,1,0:T(8,128)S(1)}, f32[1,2,40,1,128]{4,2,3,1,0:T(8,128)S(1)}, u32[]{:S(2)}, u32[]{:S(2)}) %collective-permute-start) | collective-permute-done | bytes 40992 | tf_op jit(solution)/shard_map/while/body/eval_jaxpr/ppermute | solution.py:29
  59.1 0.8 collective-permute-done.2
  60.6 1.4 fusion.39
  62.0 1.1 copy.49
  63.1 4.7 %collective-permute-start.1 = (f32[1,2,40,1,128]{4,2,3,1,0:T(8,128)S(1)}, f32[1,2,40,1,128]{4,2,3,1,0:T(8,128)S(1)}, u32[]{:S(2)}, u32[]{:S(2)}) collective-permute-start(f32[1,2,40,1,128]{4,2,3,1,0:T(8,128)S(1)} %get-tuple-element.103), channel_id=1, source_target_pairs={{2,0},{4,2},{6,4},{8,6},{10,8},{12,10},{14,12},{0,14},{3,1},{5,3},... | collective-permute-start | bytes 122888 | tf_op jit(solution)/shard_map/while/body/eval_jaxpr/ppermute | solution.py:31
  67.8 2.0 %collective-permute-done = f32[1,2,40,1,128]{4,2,3,1,0:T(8,128)S(1)} collective-permute-done((f32[1,2,40,1,128]{4,2,3,1,0:T(8,128)S(1)}, f32[1,2,40,1,128]{4,2,3,1,0:T(8,128)S(1)}, u32[]{:S(2)}, u32[]{:S(2)}) %collective-permute-start) | collective-permute-done | bytes 40992 | tf_op jit(solution)/shard_map/while/body/eval_jaxpr/ppermute | solution.py:29
  71.4 0.8 collective-permute-done.2
  72.9 1.4 fusion.39
  74.3 1.1 copy.49
  75.4 4.7 %collective-permute-start.1 = (f32[1,2,40,1,128]{4,2,3,1,0:T(8,128)S(1)}, f32[1,2,40,1,128]{4,2,3,1,0:T(8,128)S(1)}, u32[]{:S(2)}, u32[]{:S(2)}) collective-permute-start(f32[1,2,40,1,128]{4,2,3,1,0:T(8,128)S(1)} %get-tuple-element.103), channel_id=1, source_target_pairs={{2,0},{4,2},{6,4},{8,6},{10,8},{12,10},{14,12},{0,14},{3,1},{5,3},... | collective-permute-start | bytes 122888 | tf_op jit(solution)/shard_map/while/body/eval_jaxpr/ppermute | solution.py:31
  80.1 2.0 %collective-permute-done = f32[1,2,40,1,128]{4,2,3,1,0:T(8,128)S(1)} collective-permute-done((f32[1,2,40,1,128]{4,2,3,1,0:T(8,128)S(1)}, f32[1,2,40,1,128]{4,2,3,1,0:T(8,128)S(1)}, u32[]{:S(2)}, u32[]{:S(2)}) %collective-permute-start) | collective-permute-done | bytes 40992 | tf_op jit(solution)/shard_map/while/body/eval_jaxpr/ppermute | solution.py:29
  83.7 0.8 collective-permute-done.2
  85.1 1.4 fusion.39
  86.6 1.1 copy.49
  87.7 4.7 %collective-permute-start.1 = (f32[1,2,40,1,128]{4,2,3,1,0:T(8,128)S(1)}, f32[1,2,40,1,128]{4,2,3,1,0:T(8,128)S(1)}, u32[]{:S(2)}, u32[]{:S(2)}) collective-permute-start(f32[1,2,40,1,128]{4,2,3,1,0:T(8,128)S(1)} %get-tuple-element.103), channel_id=1, source_target_pairs={{2,0},{4,2},{6,4},{8,6},{10,8},{12,10},{14,12},{0,14},{3,1},{5,3},... | collective-permute-start | bytes 122888 | tf_op jit(solution)/shard_map/while/body/eval_jaxpr/ppermute | solution.py:31
  92.4 2.0 %collective-permute-done = f32[1,2,40,1,128]{4,2,3,1,0:T(8,128)S(1)} collective-permute-done((f32[1,2,40,1,128]{4,2,3,1,0:T(8,128)S(1)}, f32[1,2,40,1,128]{4,2,3,1,0:T(8,128)S(1)}, u32[]{:S(2)}, u32[]{:S(2)}) %collective-permute-start) | collective-permute-done | bytes 40992 | tf_op jit(solution)/shard_map/while/body/eval_jaxpr/ppermute | solution.py:29
  96.0 0.8 collective-permute-done.2
  97.4 1.4 fusion.39
  98.9 1.1 copy.49
  100.0 4.7 %collective-permute-start.1 = (f32[1,2,40,1,128]{4,2,3,1,0:T(8,128)S(1)}, f32[1,2,40,1,128]{4,2,3,1,0:T(8,128)S(1)}, u32[]{:S(2)}, u32[]{:S(2)}) collective-permute-start(f32[1,2,40,1,128]{4,2,3,1,0:T(8,128)S(1)} %get-tuple-element.103), channel_id=1, source_target_pairs={{2,0},{4,2},{6,4},{8,6},{10,8},{12,10},{14,12},{0,14},{3,1},{5,3},... | collective-permute-start | bytes 122888 | tf_op jit(solution)/shard_map/while/body/eval_jaxpr/ppermute | solution.py:31
  104.7 2.0 %collective-permute-done = f32[1,2,40,1,128]{4,2,3,1,0:T(8,128)S(1)} collective-permute-done((f32[1,2,40,1,128]{4,2,3,1,0:T(8,128)S(1)}, f32[1,2,40,1,128]{4,2,3,1,0:T(8,128)S(1)}, u32[]{:S(2)}, u32[]{:S(2)}) %collective-permute-start) | collective-permute-done | bytes 40992 | tf_op jit(solution)/shard_map/while/body/eval_jaxpr/ppermute | solution.py:29
  108.3 0.8 collective-permute-done.2
  109.7 1.4 fusion.39
  111.2 1.1 copy.49
  112.3 4.7 %collective-permute-start.1 = (f32[1,2,40,1,128]{4,2,3,1,0:T(8,128)S(1)}, f32[1,2,40,1,128]{4,2,3,1,0:T(8,128)S(1)}, u32[]{:S(2)}, u32[]{:S(2)}) collective-permute-start(f32[1,2,40,1,128]{4,2,3,1,0:T(8,128)S(1)} %get-tuple-element.103), channel_id=1, source_target_pairs={{2,0},{4,2},{6,4},{8,6},{10,8},{12,10},{14,12},{0,14},{3,1},{5,3},... | collective-permute-start | bytes 122888 | tf_op jit(solution)/shard_map/while/body/eval_jaxpr/ppermute | solution.py:31
  117.0 2.0 %collective-permute-done = f32[1,2,40,1,128]{4,2,3,1,0:T(8,128)S(1)} collective-permute-done((f32[1,2,40,1,128]{4,2,3,1,0:T(8,128)S(1)}, f32[1,2,40,1,128]{4,2,3,1,0:T(8,128)S(1)}, u32[]{:S(2)}, u32[]{:S(2)}) %collective-permute-start) | collective-permute-done | bytes 40992 | tf_op jit(solution)/shard_map/while/body/eval_jaxpr/ppermute | solution.py:29
  120.6 0.8 collective-permute-done.2
  122.0 1.4 fusion.39
  123.5 1.1 copy.49
  124.6 4.7 %collective-permute-start.1 = (f32[1,2,40,1,128]{4,2,3,1,0:T(8,128)S(1)}, f32[1,2,40,1,128]{4,2,3,1,0:T(8,128)S(1)}, u32[]{:S(2)}, u32[]{:S(2)}) collective-permute-start(f32[1,2,40,1,128]{4,2,3,1,0:T(8,128)S(1)} %get-tuple-element.103), channel_id=1, source_target_pairs={{2,0},{4,2},{6,4},{8,6},{10,8},{12,10},{14,12},{0,14},{3,1},{5,3},... | collective-permute-start | bytes 122888 | tf_op jit(solution)/shard_map/while/body/eval_jaxpr/ppermute | solution.py:31
  129.3 2.0 %collective-permute-done = f32[1,2,40,1,128]{4,2,3,1,0:T(8,128)S(1)} collective-permute-done((f32[1,2,40,1,128]{4,2,3,1,0:T(8,128)S(1)}, f32[1,2,40,1,128]{4,2,3,1,0:T(8,128)S(1)}, u32[]{:S(2)}, u32[]{:S(2)}) %collective-permute-start) | collective-permute-done | bytes 40992 | tf_op jit(solution)/shard_map/while/body/eval_jaxpr/ppermute | solution.py:29
  132.9 0.8 collective-permute-done.2
  134.3 1.4 fusion.39
  135.7 1.1 copy.49
  136.8 4.7 %collective-permute-start.1 = (f32[1,2,40,1,128]{4,2,3,1,0:T(8,128)S(1)}, f32[1,2,40,1,128]{4,2,3,1,0:T(8,128)S(1)}, u32[]{:S(2)}, u32[]{:S(2)}) collective-permute-start(f32[1,2,40,1,128]{4,2,3,1,0:T(8,128)S(1)} %get-tuple-element.103), channel_id=1, source_target_pairs={{2,0},{4,2},{6,4},{8,6},{10,8},{12,10},{14,12},{0,14},{3,1},{5,3},... | collective-permute-start | bytes 122888 | tf_op jit(solution)/shard_map/while/body/eval_jaxpr/ppermute | solution.py:31
  141.6 2.0 %collective-permute-done = f32[1,2,40,1,128]{4,2,3,1,0:T(8,128)S(1)} collective-permute-done((f32[1,2,40,1,128]{4,2,3,1,0:T(8,128)S(1)}, f32[1,2,40,1,128]{4,2,3,1,0:T(8,128)S(1)}, u32[]{:S(2)}, u32[]{:S(2)}) %collective-permute-start) | collective-permute-done | bytes 40992 | tf_op jit(solution)/shard_map/while/body/eval_jaxpr/ppermute | solution.py:29
  145.2 0.8 collective-permute-done.2
  146.6 1.4 fusion.39
  148.0 2.0 %copy.20 = f32[1,2,40,16,128]{4,3,2,1,0:T(8,128)} copy(f32[1,2,40,16,128]{4,2,3,1,0:T(8,128)} %get-tuple-element.32) | data formatting | bytes 1310720 | tf_op jit(solution)/shard_map/while | solution.py:99
  (166 shorter events, 22.8 us)
Async XLA Ops:
  0.0 23.4 %copy-start = (f32[2,80,80]{2,1,0:T(8,128)S(1)}, f32[2,80,80]{2,1,0:T(8,128)}, u32[]{:S(2)}) copy-start(f32[2,80,80]{2,1,0:T(8,128)} %param.8) | copy-start | bytes 153604
  0.0 7.1 %copy-start.1 = (f32[1,2,40,16,128]{4,3,2,1,0:T(8,128)S(1)}, f32[1,2,40,16,128]{4,3,2,1,0:T(8,128)}, u32[]{:S(2)}) copy-start(f32[1,2,40,16,128]{4,3,2,1,0:T(8,128)} %param.7) | copy-start | bytes 1966084
  0.8 9.1 %collective-permute-start.5 = (f32[1,128]{1,0:T(1,128)S(1)}, f32[1,128]{1,0:T(1,128)S(1)}, u32[]{:S(2)}, u32[]{:S(2)}) collective-permute-start(f32[1,128]{1,0:T(1,128)S(1)} %slice_bitcast_fusion.1), channel_id=1, source_target_pairs={{14,0},{0,2},{2,4},{4,6},{6,8},{8,10},{10,12},{12,14},{15,1},{1,3}... | collective-permute-start | bytes 1544 | tf_op jit(solution)/shard_map/ppermute | solution.py:13
  4.5 5.2 %collective-permute-start.6 = (f32[16,1]{1,0:T(8,128)S(1)}, f32[16,1]{1,0:T(8,128)S(1)}, u32[]{:S(2)}, u32[]{:S(2)}) collective-permute-start(f32[16,1]{1,0:T(8,128)S(1)} %slice.63), channel_id=1, source_target_pairs={{0,1},{2,3},{4,5},{6,7},{8,9},{10,11},{12,13},{14,15},{16,17},{18,... | collective-permute-start | bytes 200 | tf_op jit(solution)/shard_map/ppermute | solution.py:19
  7.3 16.1 %collective-permute-start.4 = (f32[1,2,40,16,128]{4,2,3,1,0:T(8,128)S(1)}, f32[1,2,40,16,128]{4,2,3,1,0:T(8,128)S(1)}, u32[]{:S(2)}, u32[]{:S(2)}) collective-permute-start(f32[1,2,40,16,128]{4,2,3,1,0:T(8,128)S(1)} %copy_multiply_fusion), channel_id=1, source_target_pairs={{0,16},{16,0},{1,17},{17,1},{2,18},{18,2},{3,19},{19,3},{4,20},{20... | collective-permute-start | bytes 1966088 | tf_op jit(solution)/shard_map/ppermute | solution.py:58
  9.0 0.7 copy-start.2
  26.3 6.7 %collective-permute-start = (f32[1,2,40,1,128]{4,2,3,1,0:T(8,128)S(1)}, f32[1,2,40,1,128]{4,2,3,1,0:T(8,128)S(1)}, u32[]{:S(2)}, u32[]{:S(2)}) collective-permute-start(f32[1,2,40,1,128]{4,2,3,1,0:T(8,128)S(1)} %get-tuple-element.102), channel_id=1, source_target_pairs={{0,2},{2,4},{4,6},{6,8},{8,10},{10,12},{12,14},{14,0},{1,3},{3,5},... | collective-permute-start | bytes 122888 | tf_op jit(solution)/shard_map/while/body/eval_jaxpr/ppermute | solution.py:29
  27.8 5.2 %collective-permute-start.1 = (f32[1,2,40,1,128]{4,2,3,1,0:T(8,128)S(1)}, f32[1,2,40,1,128]{4,2,3,1,0:T(8,128)S(1)}, u32[]{:S(2)}, u32[]{:S(2)}) collective-permute-start(f32[1,2,40,1,128]{4,2,3,1,0:T(8,128)S(1)} %get-tuple-element.103), channel_id=1, source_target_pairs={{2,0},{4,2},{6,4},{8,6},{10,8},{12,10},{14,12},{0,14},{3,1},{5,3},... | collective-permute-start | bytes 122888 | tf_op jit(solution)/shard_map/while/body/eval_jaxpr/ppermute | solution.py:31
  33.9 1.8 %collective-permute-start.3 = (f32[1,2,40,18,1]{2,1,4,3,0:T(2,128)S(1)}, f32[1,2,40,18,1]{2,1,4,3,0:T(2,128)S(1)}, u32[]{:S(2)}, u32[]{:S(2)}) collective-permute-start(f32[1,2,40,18,1]{2,1,4,3,0:T(2,128)S(1)} %copy.36), channel_id=1, source_target_pairs={{1,0},{0,1},{3,2},{2,3},{5,4},{4,5},{7,6},{6,7},{9,8},{8,9},{11,10... | collective-permute-start | bytes 17288 | tf_op jit(solution)/shard_map/while/body/eval_jaxpr/ppermute | solution.py:31
  34.0 1.3 collective-permute-start.2
  38.5 6.7 %collective-permute-start = (f32[1,2,40,1,128]{4,2,3,1,0:T(8,128)S(1)}, f32[1,2,40,1,128]{4,2,3,1,0:T(8,128)S(1)}, u32[]{:S(2)}, u32[]{:S(2)}) collective-permute-start(f32[1,2,40,1,128]{4,2,3,1,0:T(8,128)S(1)} %get-tuple-element.102), channel_id=1, source_target_pairs={{0,2},{2,4},{4,6},{6,8},{8,10},{10,12},{12,14},{14,0},{1,3},{3,5},... | collective-permute-start | bytes 122888 | tf_op jit(solution)/shard_map/while/body/eval_jaxpr/ppermute | solution.py:29
  39.7 5.6 %collective-permute-start.1 = (f32[1,2,40,1,128]{4,2,3,1,0:T(8,128)S(1)}, f32[1,2,40,1,128]{4,2,3,1,0:T(8,128)S(1)}, u32[]{:S(2)}, u32[]{:S(2)}) collective-permute-start(f32[1,2,40,1,128]{4,2,3,1,0:T(8,128)S(1)} %get-tuple-element.103), channel_id=1, source_target_pairs={{2,0},{4,2},{6,4},{8,6},{10,8},{12,10},{14,12},{0,14},{3,1},{5,3},... | collective-permute-start | bytes 122888 | tf_op jit(solution)/shard_map/while/body/eval_jaxpr/ppermute | solution.py:31
  46.2 1.8 %collective-permute-start.3 = (f32[1,2,40,18,1]{2,1,4,3,0:T(2,128)S(1)}, f32[1,2,40,18,1]{2,1,4,3,0:T(2,128)S(1)}, u32[]{:S(2)}, u32[]{:S(2)}) collective-permute-start(f32[1,2,40,18,1]{2,1,4,3,0:T(2,128)S(1)} %copy.36), channel_id=1, source_target_pairs={{1,0},{0,1},{3,2},{2,3},{5,4},{4,5},{7,6},{6,7},{9,8},{8,9},{11,10... | collective-permute-start | bytes 17288 | tf_op jit(solution)/shard_map/while/body/eval_jaxpr/ppermute | solution.py:31
  46.3 1.3 collective-permute-start.2
  50.8 6.7 %collective-permute-start = (f32[1,2,40,1,128]{4,2,3,1,0:T(8,128)S(1)}, f32[1,2,40,1,128]{4,2,3,1,0:T(8,128)S(1)}, u32[]{:S(2)}, u32[]{:S(2)}) collective-permute-start(f32[1,2,40,1,128]{4,2,3,1,0:T(8,128)S(1)} %get-tuple-element.102), channel_id=1, source_target_pairs={{0,2},{2,4},{4,6},{6,8},{8,10},{10,12},{12,14},{14,0},{1,3},{3,5},... | collective-permute-start | bytes 122888 | tf_op jit(solution)/shard_map/while/body/eval_jaxpr/ppermute | solution.py:29
  50.8 6.7 %collective-permute-start.1 = (f32[1,2,40,1,128]{4,2,3,1,0:T(8,128)S(1)}, f32[1,2,40,1,128]{4,2,3,1,0:T(8,128)S(1)}, u32[]{:S(2)}, u32[]{:S(2)}) collective-permute-start(f32[1,2,40,1,128]{4,2,3,1,0:T(8,128)S(1)} %get-tuple-element.103), channel_id=1, source_target_pairs={{2,0},{4,2},{6,4},{8,6},{10,8},{12,10},{14,12},{0,14},{3,1},{5,3},... | collective-permute-start | bytes 122888 | tf_op jit(solution)/shard_map/while/body/eval_jaxpr/ppermute | solution.py:31
  58.5 1.8 %collective-permute-start.3 = (f32[1,2,40,18,1]{2,1,4,3,0:T(2,128)S(1)}, f32[1,2,40,18,1]{2,1,4,3,0:T(2,128)S(1)}, u32[]{:S(2)}, u32[]{:S(2)}) collective-permute-start(f32[1,2,40,18,1]{2,1,4,3,0:T(2,128)S(1)} %copy.36), channel_id=1, source_target_pairs={{1,0},{0,1},{3,2},{2,3},{5,4},{4,5},{7,6},{6,7},{9,8},{8,9},{11,10... | collective-permute-start | bytes 17288 | tf_op jit(solution)/shard_map/while/body/eval_jaxpr/ppermute | solution.py:31
  58.6 1.3 collective-permute-start.2
  63.1 6.7 %collective-permute-start = (f32[1,2,40,1,128]{4,2,3,1,0:T(8,128)S(1)}, f32[1,2,40,1,128]{4,2,3,1,0:T(8,128)S(1)}, u32[]{:S(2)}, u32[]{:S(2)}) collective-permute-start(f32[1,2,40,1,128]{4,2,3,1,0:T(8,128)S(1)} %get-tuple-element.102), channel_id=1, source_target_pairs={{0,2},{2,4},{4,6},{6,8},{8,10},{10,12},{12,14},{14,0},{1,3},{3,5},... | collective-permute-start | bytes 122888 | tf_op jit(solution)/shard_map/while/body/eval_jaxpr/ppermute | solution.py:29
  63.1 6.8 %collective-permute-start.1 = (f32[1,2,40,1,128]{4,2,3,1,0:T(8,128)S(1)}, f32[1,2,40,1,128]{4,2,3,1,0:T(8,128)S(1)}, u32[]{:S(2)}, u32[]{:S(2)}) collective-permute-start(f32[1,2,40,1,128]{4,2,3,1,0:T(8,128)S(1)} %get-tuple-element.103), channel_id=1, source_target_pairs={{2,0},{4,2},{6,4},{8,6},{10,8},{12,10},{14,12},{0,14},{3,1},{5,3},... | collective-permute-start | bytes 122888 | tf_op jit(solution)/shard_map/while/body/eval_jaxpr/ppermute | solution.py:31
  70.8 1.8 %collective-permute-start.3 = (f32[1,2,40,18,1]{2,1,4,3,0:T(2,128)S(1)}, f32[1,2,40,18,1]{2,1,4,3,0:T(2,128)S(1)}, u32[]{:S(2)}, u32[]{:S(2)}) collective-permute-start(f32[1,2,40,18,1]{2,1,4,3,0:T(2,128)S(1)} %copy.36), channel_id=1, source_target_pairs={{1,0},{0,1},{3,2},{2,3},{5,4},{4,5},{7,6},{6,7},{9,8},{8,9},{11,10... | collective-permute-start | bytes 17288 | tf_op jit(solution)/shard_map/while/body/eval_jaxpr/ppermute | solution.py:31
  70.9 1.3 collective-permute-start.2
  75.4 6.7 %collective-permute-start = (f32[1,2,40,1,128]{4,2,3,1,0:T(8,128)S(1)}, f32[1,2,40,1,128]{4,2,3,1,0:T(8,128)S(1)}, u32[]{:S(2)}, u32[]{:S(2)}) collective-permute-start(f32[1,2,40,1,128]{4,2,3,1,0:T(8,128)S(1)} %get-tuple-element.102), channel_id=1, source_target_pairs={{0,2},{2,4},{4,6},{6,8},{8,10},{10,12},{12,14},{14,0},{1,3},{3,5},... | collective-permute-start | bytes 122888 | tf_op jit(solution)/shard_map/while/body/eval_jaxpr/ppermute | solution.py:29
  75.4 6.7 %collective-permute-start.1 = (f32[1,2,40,1,128]{4,2,3,1,0:T(8,128)S(1)}, f32[1,2,40,1,128]{4,2,3,1,0:T(8,128)S(1)}, u32[]{:S(2)}, u32[]{:S(2)}) collective-permute-start(f32[1,2,40,1,128]{4,2,3,1,0:T(8,128)S(1)} %get-tuple-element.103), channel_id=1, source_target_pairs={{2,0},{4,2},{6,4},{8,6},{10,8},{12,10},{14,12},{0,14},{3,1},{5,3},... | collective-permute-start | bytes 122888 | tf_op jit(solution)/shard_map/while/body/eval_jaxpr/ppermute | solution.py:31
  83.1 1.8 %collective-permute-start.3 = (f32[1,2,40,18,1]{2,1,4,3,0:T(2,128)S(1)}, f32[1,2,40,18,1]{2,1,4,3,0:T(2,128)S(1)}, u32[]{:S(2)}, u32[]{:S(2)}) collective-permute-start(f32[1,2,40,18,1]{2,1,4,3,0:T(2,128)S(1)} %copy.36), channel_id=1, source_target_pairs={{1,0},{0,1},{3,2},{2,3},{5,4},{4,5},{7,6},{6,7},{9,8},{8,9},{11,10... | collective-permute-start | bytes 17288 | tf_op jit(solution)/shard_map/while/body/eval_jaxpr/ppermute | solution.py:31
  83.1 1.3 collective-permute-start.2
  87.7 6.7 %collective-permute-start = (f32[1,2,40,1,128]{4,2,3,1,0:T(8,128)S(1)}, f32[1,2,40,1,128]{4,2,3,1,0:T(8,128)S(1)}, u32[]{:S(2)}, u32[]{:S(2)}) collective-permute-start(f32[1,2,40,1,128]{4,2,3,1,0:T(8,128)S(1)} %get-tuple-element.102), channel_id=1, source_target_pairs={{0,2},{2,4},{4,6},{6,8},{8,10},{10,12},{12,14},{14,0},{1,3},{3,5},... | collective-permute-start | bytes 122888 | tf_op jit(solution)/shard_map/while/body/eval_jaxpr/ppermute | solution.py:29
  87.7 6.8 %collective-permute-start.1 = (f32[1,2,40,1,128]{4,2,3,1,0:T(8,128)S(1)}, f32[1,2,40,1,128]{4,2,3,1,0:T(8,128)S(1)}, u32[]{:S(2)}, u32[]{:S(2)}) collective-permute-start(f32[1,2,40,1,128]{4,2,3,1,0:T(8,128)S(1)} %get-tuple-element.103), channel_id=1, source_target_pairs={{2,0},{4,2},{6,4},{8,6},{10,8},{12,10},{14,12},{0,14},{3,1},{5,3},... | collective-permute-start | bytes 122888 | tf_op jit(solution)/shard_map/while/body/eval_jaxpr/ppermute | solution.py:31
  95.4 1.8 %collective-permute-start.3 = (f32[1,2,40,18,1]{2,1,4,3,0:T(2,128)S(1)}, f32[1,2,40,18,1]{2,1,4,3,0:T(2,128)S(1)}, u32[]{:S(2)}, u32[]{:S(2)}) collective-permute-start(f32[1,2,40,18,1]{2,1,4,3,0:T(2,128)S(1)} %copy.36), channel_id=1, source_target_pairs={{1,0},{0,1},{3,2},{2,3},{5,4},{4,5},{7,6},{6,7},{9,8},{8,9},{11,10... | collective-permute-start | bytes 17288 | tf_op jit(solution)/shard_map/while/body/eval_jaxpr/ppermute | solution.py:31
  95.4 1.3 collective-permute-start.2
  100.0 6.7 %collective-permute-start = (f32[1,2,40,1,128]{4,2,3,1,0:T(8,128)S(1)}, f32[1,2,40,1,128]{4,2,3,1,0:T(8,128)S(1)}, u32[]{:S(2)}, u32[]{:S(2)}) collective-permute-start(f32[1,2,40,1,128]{4,2,3,1,0:T(8,128)S(1)} %get-tuple-element.102), channel_id=1, source_target_pairs={{0,2},{2,4},{4,6},{6,8},{8,10},{10,12},{12,14},{14,0},{1,3},{3,5},... | collective-permute-start | bytes 122888 | tf_op jit(solution)/shard_map/while/body/eval_jaxpr/ppermute | solution.py:29
  100.0 6.7 %collective-permute-start.1 = (f32[1,2,40,1,128]{4,2,3,1,0:T(8,128)S(1)}, f32[1,2,40,1,128]{4,2,3,1,0:T(8,128)S(1)}, u32[]{:S(2)}, u32[]{:S(2)}) collective-permute-start(f32[1,2,40,1,128]{4,2,3,1,0:T(8,128)S(1)} %get-tuple-element.103), channel_id=1, source_target_pairs={{2,0},{4,2},{6,4},{8,6},{10,8},{12,10},{14,12},{0,14},{3,1},{5,3},... | collective-permute-start | bytes 122888 | tf_op jit(solution)/shard_map/while/body/eval_jaxpr/ppermute | solution.py:31
  107.6 1.8 %collective-permute-start.3 = (f32[1,2,40,18,1]{2,1,4,3,0:T(2,128)S(1)}, f32[1,2,40,18,1]{2,1,4,3,0:T(2,128)S(1)}, u32[]{:S(2)}, u32[]{:S(2)}) collective-permute-start(f32[1,2,40,18,1]{2,1,4,3,0:T(2,128)S(1)} %copy.36), channel_id=1, source_target_pairs={{1,0},{0,1},{3,2},{2,3},{5,4},{4,5},{7,6},{6,7},{9,8},{8,9},{11,10... | collective-permute-start | bytes 17288 | tf_op jit(solution)/shard_map/while/body/eval_jaxpr/ppermute | solution.py:31
  107.7 1.3 collective-permute-start.2
  112.3 6.7 %collective-permute-start = (f32[1,2,40,1,128]{4,2,3,1,0:T(8,128)S(1)}, f32[1,2,40,1,128]{4,2,3,1,0:T(8,128)S(1)}, u32[]{:S(2)}, u32[]{:S(2)}) collective-permute-start(f32[1,2,40,1,128]{4,2,3,1,0:T(8,128)S(1)} %get-tuple-element.102), channel_id=1, source_target_pairs={{0,2},{2,4},{4,6},{6,8},{8,10},{10,12},{12,14},{14,0},{1,3},{3,5},... | collective-permute-start | bytes 122888 | tf_op jit(solution)/shard_map/while/body/eval_jaxpr/ppermute | solution.py:29
  112.3 6.8 %collective-permute-start.1 = (f32[1,2,40,1,128]{4,2,3,1,0:T(8,128)S(1)}, f32[1,2,40,1,128]{4,2,3,1,0:T(8,128)S(1)}, u32[]{:S(2)}, u32[]{:S(2)}) collective-permute-start(f32[1,2,40,1,128]{4,2,3,1,0:T(8,128)S(1)} %get-tuple-element.103), channel_id=1, source_target_pairs={{2,0},{4,2},{6,4},{8,6},{10,8},{12,10},{14,12},{0,14},{3,1},{5,3},... | collective-permute-start | bytes 122888 | tf_op jit(solution)/shard_map/while/body/eval_jaxpr/ppermute | solution.py:31
  119.9 1.8 %collective-permute-start.3 = (f32[1,2,40,18,1]{2,1,4,3,0:T(2,128)S(1)}, f32[1,2,40,18,1]{2,1,4,3,0:T(2,128)S(1)}, u32[]{:S(2)}, u32[]{:S(2)}) collective-permute-start(f32[1,2,40,18,1]{2,1,4,3,0:T(2,128)S(1)} %copy.36), channel_id=1, source_target_pairs={{1,0},{0,1},{3,2},{2,3},{5,4},{4,5},{7,6},{6,7},{9,8},{8,9},{11,10... | collective-permute-start | bytes 17288 | tf_op jit(solution)/shard_map/while/body/eval_jaxpr/ppermute | solution.py:31
  120.0 1.3 collective-permute-start.2
  124.6 6.7 %collective-permute-start = (f32[1,2,40,1,128]{4,2,3,1,0:T(8,128)S(1)}, f32[1,2,40,1,128]{4,2,3,1,0:T(8,128)S(1)}, u32[]{:S(2)}, u32[]{:S(2)}) collective-permute-start(f32[1,2,40,1,128]{4,2,3,1,0:T(8,128)S(1)} %get-tuple-element.102), channel_id=1, source_target_pairs={{0,2},{2,4},{4,6},{6,8},{8,10},{10,12},{12,14},{14,0},{1,3},{3,5},... | collective-permute-start | bytes 122888 | tf_op jit(solution)/shard_map/while/body/eval_jaxpr/ppermute | solution.py:29
  124.6 6.7 %collective-permute-start.1 = (f32[1,2,40,1,128]{4,2,3,1,0:T(8,128)S(1)}, f32[1,2,40,1,128]{4,2,3,1,0:T(8,128)S(1)}, u32[]{:S(2)}, u32[]{:S(2)}) collective-permute-start(f32[1,2,40,1,128]{4,2,3,1,0:T(8,128)S(1)} %get-tuple-element.103), channel_id=1, source_target_pairs={{2,0},{4,2},{6,4},{8,6},{10,8},{12,10},{14,12},{0,14},{3,1},{5,3},... | collective-permute-start | bytes 122888 | tf_op jit(solution)/shard_map/while/body/eval_jaxpr/ppermute | solution.py:31
  132.2 1.8 %collective-permute-start.3 = (f32[1,2,40,18,1]{2,1,4,3,0:T(2,128)S(1)}, f32[1,2,40,18,1]{2,1,4,3,0:T(2,128)S(1)}, u32[]{:S(2)}, u32[]{:S(2)}) collective-permute-start(f32[1,2,40,18,1]{2,1,4,3,0:T(2,128)S(1)} %copy.36), channel_id=1, source_target_pairs={{1,0},{0,1},{3,2},{2,3},{5,4},{4,5},{7,6},{6,7},{9,8},{8,9},{11,10... | collective-permute-start | bytes 17288 | tf_op jit(solution)/shard_map/while/body/eval_jaxpr/ppermute | solution.py:31
  132.3 1.3 collective-permute-start.2
  136.8 6.7 %collective-permute-start = (f32[1,2,40,1,128]{4,2,3,1,0:T(8,128)S(1)}, f32[1,2,40,1,128]{4,2,3,1,0:T(8,128)S(1)}, u32[]{:S(2)}, u32[]{:S(2)}) collective-permute-start(f32[1,2,40,1,128]{4,2,3,1,0:T(8,128)S(1)} %get-tuple-element.102), channel_id=1, source_target_pairs={{0,2},{2,4},{4,6},{6,8},{8,10},{10,12},{12,14},{14,0},{1,3},{3,5},... | collective-permute-start | bytes 122888 | tf_op jit(solution)/shard_map/while/body/eval_jaxpr/ppermute | solution.py:29
  136.8 6.8 %collective-permute-start.1 = (f32[1,2,40,1,128]{4,2,3,1,0:T(8,128)S(1)}, f32[1,2,40,1,128]{4,2,3,1,0:T(8,128)S(1)}, u32[]{:S(2)}, u32[]{:S(2)}) collective-permute-start(f32[1,2,40,1,128]{4,2,3,1,0:T(8,128)S(1)} %get-tuple-element.103), channel_id=1, source_target_pairs={{2,0},{4,2},{6,4},{8,6},{10,8},{12,10},{14,12},{0,14},{3,1},{5,3},... | collective-permute-start | bytes 122888 | tf_op jit(solution)/shard_map/while/body/eval_jaxpr/ppermute | solution.py:31
  144.5 1.8 %collective-permute-start.3 = (f32[1,2,40,18,1]{2,1,4,3,0:T(2,128)S(1)}, f32[1,2,40,18,1]{2,1,4,3,0:T(2,128)S(1)}, u32[]{:S(2)}, u32[]{:S(2)}) collective-permute-start(f32[1,2,40,18,1]{2,1,4,3,0:T(2,128)S(1)} %copy.36), channel_id=1, source_target_pairs={{1,0},{0,1},{3,2},{2,3},{5,4},{4,5},{7,6},{6,7},{9,8},{8,9},{11,10... | collective-permute-start | bytes 17288 | tf_op jit(solution)/shard_map/while/body/eval_jaxpr/ppermute | solution.py:31
  144.6 1.3 collective-permute-start.2
